TPU v7x, 256 devices: a whole 4x4x8 slice. The times are simulated.
256 devices in a mesh: tm: 8 (over z_hi, core), space: 32 (over y, x, z_lo).
Axes of the slice: x: 4, y: 4, z: 8 (z_hi: 4, z_lo: 2; z = z_hi * 2 + z_lo), core: 2. Of those that a mesh axis runs over, the one named last changes fastest.
Arguments:
- pressure: float32 [8, 2, 8, 512, 2048], P('tm', None, None, 'space'), may hold values from -6 to 6
- mobility: float32 [8, 2, 8, 512, 2048], P('tm', None, None, 'space'), may hold values from 0.05 to 1
- capacity: float32 [8, 2, 8, 512, 2048], P('tm', None, None, 'space'), may hold values from 0.5 to 2
- misfit_weight: float32 [8, 8, 512, 2048], P('tm', None, 'space'), may hold values from 0.2 to 1
- log_permeability: float32 [512, 2048], P('space'), may hold values from -3 to 3
- direction: float32 [512, 2048], P('space'), may hold values from -9 to 9
Outputs:
- hessian_product: float32 [512, 2048], P('space')
- curvature: float32 [], replicated
All inputs are finite; a program needn't handle non-finite values.
Results may differ from a plain program's by a relative error of at most 0.00002.
Values sent between devices are 32-bit elements; how exact they have to be, the bound alone decides.
A program may use at most 64 MiB of HBM per device.

v0:
```python
import jax
import jax.numpy as jnp
from jax import lax
from jax.sharding import PartitionSpec as P

LAYERS = 8
STEPS = 2


def extended(cells, sides, width):
    for axis, dim in sides:
        count = lax.axis_size(axis)
        ends = count - 1
        head = lax.slice_in_dim(cells, 0, width, axis=dim)
        tail = lax.slice_in_dim(cells, cells.shape[dim] - width, cells.shape[dim], axis=dim)
        cells = jnp.concatenate(
            [
                lax.ppermute(tail, axis, [(i, (i + 1) % count) for i in range(ends)]),
                cells,
                lax.ppermute(head, axis, [((i + 1) % count, i) for i in range(ends)]),
            ],
            axis=dim,
        )
    return cells


def shards(pressure, mobility, capacity, misfit_weight, log_permeability, direction):
    position = lax.axis_index("space")
    devices = lax.axis_size("space")
    height = pressure.shape[3]
    conduct = jnp.exp(log_permeability)
    scaled = conduct * direction
    pressure_w = pressure[0]
    mobility_w = mobility[0]
    capacity_w = capacity[0]
    weight_w = misfit_weight[0]
    face_y = (
        0.5
        * (mobility_w[..., 1:] + mobility_w[..., :-1])
        * (pressure_w[..., 1:] - pressure_w[..., :-1])
    )
    flux_y = 0.5 * (scaled[:, 1:] + scaled[:, :-1]) * face_y
    padded_y = jnp.pad(flux_y, ((0, 0), (0, 0), (0, 0), (1, 1)))
    change_y = padded_y[..., 1:] - padded_y[..., :-1]
    stacked = jnp.stack((pressure_w, mobility_w))
    padded = extended(stacked, (("space", 3),), 1)
    face_x = (
        0.5
        * (padded[1, ..., 1:, :] + padded[1, ..., :-1, :])
        * (padded[0, ..., 1:, :] - padded[0, ..., :-1, :])
    )
    face_index = lax.iota(jnp.int32, height + 1)
    keep_face = ((face_index > 0) | (position > 0)) & (
        (face_index < height) | (position < devices - 1)
    )
    face_x = face_x * keep_face.astype(jnp.float32)[:, None]
    scaled_ext = extended(scaled, (("space", 0),), 1)
    flux_x = 0.5 * (scaled_ext[1:] + scaled_ext[:-1]) * face_x
    change = flux_x[..., 1:, :] - flux_x[..., :-1, :] + change_y
    tangent = change / capacity_w
    adjoint = weight_w * tangent / capacity_w
    adjoint_ext = extended(adjoint, (("space", 2),), 1)
    term_x = face_x * (adjoint_ext[..., :-1, :] - adjoint_ext[..., 1:, :])
    summed_x = jnp.sum(term_x, axis=(0, 1))
    column_x = summed_x[1:] + summed_x[:-1]
    term_y = face_y * (adjoint[..., :-1] - adjoint[..., 1:])
    padded_ty = jnp.pad(term_y, ((0, 0), (0, 0), (0, 0), (1, 1)))
    column_y = jnp.sum(padded_ty[..., 1:] + padded_ty[..., :-1], axis=(0, 1))
    windows = lax.axis_size("tm")
    share = 0.5 * conduct * (column_x + column_y) / (LAYERS * STEPS * windows)
    hessian_product = lax.psum(share, "tm")
    cells = height * devices * direction.shape[1]
    curvature = lax.psum(jnp.sum(direction * hessian_product), "space") / cells
    return (hessian_product, curvature)


def solution(mesh):
    placed = (
        P("tm", None, None, "space", None),
        P("tm", None, None, "space", None),
        P("tm", None, None, "space", None),
        P("tm", None, "space", None),
        P("space", None),
        P("space", None),
    )
    return jax.shard_map(
        shards, mesh=mesh, in_specs=placed, out_specs=(P("space", None), P()), check_vma=False
    )
```

profile of v0, /device:TPU:0, one launch (start us, length us, event | category | flops | bytes accessed | tf_op | source)
XLA Modules:
  0.0 224.2 jit_solution(5592595358356381332)
XLA Ops:
  7.2 1.1 exponential_multiply_fusion
  8.4 1.3 collective-permute-start.2
  9.7 4.5 %collective-permute-start.3 = (f32[1,2048]{1,0:T(1,128)S(1)}, f32[1,2048]{1,0:T(1,128)S(1)}, u32[]{:S(2)}, u32[]{:S(2)}) collective-permute-start(f32[1,2048]{1,0:T(1,128)S(1)} %get-tuple-element.10), channel_id=1, source_target_pairs={{0,1},{1,2},{2,3},{3,4},{4,5},{5,6},{6,7},{7,8},{8,9},{9,10},{10,1... | collective-permute-start | bytes 24584 | tf_op jit(solution)/shard_map/ppermute | solution.py:18
  14.2 1.7 constant_dynamic-update-slice_fusion.1
  16.0 0.2 constant_dynamic-update-slice_fusion
  16.2 1.9 copy-done.2
  18.2 0.4 fusion.27
  18.6 1.3 collective-permute-start
  19.9 4.6 %collective-permute-start.1 = (f32[2,2,8,1,2048]{4,3,2,1,0:T(1,128)S(1)}, f32[2,2,8,1,2048]{4,3,2,1,0:T(1,128)S(1)}, u32[]{:S(2)}, u32[]{:S(2)}) collective-permute-start(f32[2,2,8,1,2048]{4,3,2,1,0:T(1,128)S(1)} %get-tuple-element.7), channel_id=1, source_target_pairs={{0,1},{1,2},{2,3},{3,4},{4,5},{5,6},{6,7},{7,8},{8,9},{9,10},{10,1... | collective-permute-start | bytes 786440 | tf_op jit(solution)/shard_map/ppermute | solution.py:18
  24.6 3.5 %broadcast_multiply_fusion.1 = (f32[2,8,16,2047]{3,2,1,0:T(8,128)S(1)}, f32[2,8,16,2047]{3,2,1,0:T(8,128)S(1)}) fusion(f32[16,2047]{1,0:T(8,128)S(1)} %fusion.24, f32[2,8,16,2048]{3,2,1,0:T(8,128)S(1)} %bitcast.10, f32[2,8,16,2048]{3,2,1,0:T(8,128)} %bitcast.11), kind=kLoop, calls=%fused_computation.36 | loop fusion | flops 2620160 | bytes 12707776 | tf_op jit(solution)/shard_map/mul | solution.py:42
  28.3 0.4 collective-permute-done
  28.6 1.6 broadcast_multiply_fusion
  30.2 1.1 fusion.14
  31.6 5.8 %collective-permute-start.4 = (f32[2,8,1,2048]{3,2,1,0:T(1,128)S(1)}, f32[2,8,1,2048]{3,2,1,0:T(1,128)S(1)}, u32[]{:S(2)}, u32[]{:S(2)}) collective-permute-start(f32[2,8,1,2048]{3,2,1,0:T(1,128)S(1)} %get-tuple-element.9), channel_id=1, source_target_pairs={{0,1},{1,2},{2,3},{3,4},{4,5},{5,6},{6,7},{7,8},{8,9},{9,10},{10,1... | collective-permute-start | bytes 393224 | tf_op jit(solution)/shard_map/ppermute | solution.py:18
  37.3 1.3 collective-permute-start.5
  38.6 0.8 fusion.17
  39.4 0.6 fusion.16
  40.1 6.2 %collective-permute-done.5 = f32[2,8,1,2048]{3,2,1,0:T(1,128)S(1)} collective-permute-done((f32[2,8,1,2048]{3,2,1,0:T(1,128)S(1)}, f32[2,8,1,2048]{3,2,1,0:T(1,128)S(1)}, u32[]{:S(2)}, u32[]{:S(2)}) %collective-permute-start.5) | collective-permute-done | bytes 131104 | tf_op jit(solution)/shard_map/ppermute | solution.py:20
  46.2 0.8 fusion.9
  47.1 0.7 fusion.23
  47.9 81.8 %all-reduce.4.cloned.1.call-done = f32[16,2048]{1,0:T(8,128)} async-done(((f32[16,2048]{1,0:T(8,128)}), f32[16,2048]{1,0:T(8,128)}) %all-reduce.4.cloned.1.call-update) | async-done | bytes 131088 | tf_op jit(solution)/shard_map/psum | solution.py:71
  129.7 1.5 multiply_reduce_fusion
  131.2 82.8 %psum.15 = f32[]{:T(128)} all-reduce(f32[]{:T(128)} %multiply_reduce_fusion), channel_id=1, replica_groups=mesh['tm'=8,'space'=32] {'space'}, use_global_device_ids=true, to_apply=%region_4.5 | all-reduce | flops 1 | bytes 8 | tf_op jit(solution)/shard_map/psum | solution.py:73
  214.7 1.6 copy.10
  (26 shorter events, 0.6 us)
Async XLA Ops:
  7.2 122.5 %all-reduce.4.cloned.1.call-start = ((), (), s32[]{:S(2)}) async-start(), calls=%async_computation | async-start | bytes 262144 | tf_op jit(solution)/shard_map/psum | solution.py:71
  7.2 8.8 %copy-start.1 = (f32[1,2,8,16,2048]{4,3,2,1,0:T(8,128)S(1)}, f32[1,2,8,16,2048]{4,3,2,1,0:T(8,128)}, u32[]{:S(2)}) copy-start(f32[1,2,8,16,2048]{4,3,2,1,0:T(8,128)} %param.7) | copy-start | bytes 6291460
  8.4 19.8 %collective-permute-start.2 = (f32[1,2048]{1,0:T(1,128)S(1)}, f32[1,2048]{1,0:T(1,128)S(1)}, u32[]{:S(2)}, u32[]{:S(2)}) collective-permute-start(f32[1,2048]{1,0:T(1,128)S(1)} %get-tuple-element.11), channel_id=1, source_target_pairs={{1,0},{2,1},{3,2},{4,3},{5,4},{6,5},{7,6},{8,7},{9,8},{10,9},{11,1... | collective-permute-start | bytes 24584 | tf_op jit(solution)/shard_map/ppermute | solution.py:20
  9.7 18.5 %collective-permute-start.3 = (f32[1,2048]{1,0:T(1,128)S(1)}, f32[1,2048]{1,0:T(1,128)S(1)}, u32[]{:S(2)}, u32[]{:S(2)}) collective-permute-start(f32[1,2048]{1,0:T(1,128)S(1)} %get-tuple-element.10), channel_id=1, source_target_pairs={{0,1},{1,2},{2,3},{3,4},{4,5},{5,6},{6,7},{7,8},{8,9},{9,10},{10,1... | collective-permute-start | bytes 24584 | tf_op jit(solution)/shard_map/ppermute | solution.py:18
  16.0 8.6 %copy-start = (f32[1,2,8,16,2048]{4,3,2,1,0:T(8,128)S(1)}, f32[1,2,8,16,2048]{4,3,2,1,0:T(8,128)}, u32[]{:S(2)}) copy-start(f32[1,2,8,16,2048]{4,3,2,1,0:T(8,128)} %param.6) | copy-start | bytes 6291460
  16.2 1.9 copy-start.2
  18.6 10.0 %collective-permute-start = (f32[2,2,8,1,2048]{4,3,2,1,0:T(1,128)S(1)}, f32[2,2,8,1,2048]{4,3,2,1,0:T(1,128)S(1)}, u32[]{:S(2)}, u32[]{:S(2)}) collective-permute-start(f32[2,2,8,1,2048]{4,3,2,1,0:T(1,128)S(1)} %get-tuple-element.6), channel_id=1, source_target_pairs={{1,0},{2,1},{3,2},{4,3},{5,4},{6,5},{7,6},{8,7},{9,8},{10,9},{11,1... | collective-permute-start | bytes 786440 | tf_op jit(solution)/shard_map/ppermute | solution.py:20
  19.9 8.7 %collective-permute-start.1 = (f32[2,2,8,1,2048]{4,3,2,1,0:T(1,128)S(1)}, f32[2,2,8,1,2048]{4,3,2,1,0:T(1,128)S(1)}, u32[]{:S(2)}, u32[]{:S(2)}) collective-permute-start(f32[2,2,8,1,2048]{4,3,2,1,0:T(1,128)S(1)} %get-tuple-element.7), channel_id=1, source_target_pairs={{0,1},{1,2},{2,3},{3,4},{4,5},{5,6},{6,7},{7,8},{8,9},{9,10},{10,1... | collective-permute-start | bytes 786440 | tf_op jit(solution)/shard_map/ppermute | solution.py:18
  24.6 4.0 %copy-start.3 = (f32[2,2,8,16,2048]{4,3,2,1,0:T(8,128)S(1)}, f32[2,2,8,16,2048]{4,3,2,1,0:T(8,128)}, u32[]{:S(2)}) copy-start(f32[2,2,8,16,2048]{4,3,2,1,0:T(8,128)} %copy-done.2) | copy-start | bytes 12582916
  28.2 2.0 copy-start.4
  28.2 2.0 copy-start.5
  31.6 8.5 %collective-permute-start.4 = (f32[2,8,1,2048]{3,2,1,0:T(1,128)S(1)}, f32[2,8,1,2048]{3,2,1,0:T(1,128)S(1)}, u32[]{:S(2)}, u32[]{:S(2)}) collective-permute-start(f32[2,8,1,2048]{3,2,1,0:T(1,128)S(1)} %get-tuple-element.9), channel_id=1, source_target_pairs={{0,1},{1,2},{2,3},{3,4},{4,5},{5,6},{6,7},{7,8},{8,9},{9,10},{10,1... | collective-permute-start | bytes 393224 | tf_op jit(solution)/shard_map/ppermute | solution.py:18
  37.3 8.9 %collective-permute-start.5 = (f32[2,8,1,2048]{3,2,1,0:T(1,128)S(1)}, f32[2,8,1,2048]{3,2,1,0:T(1,128)S(1)}, u32[]{:S(2)}, u32[]{:S(2)}) collective-permute-start(f32[2,8,1,2048]{3,2,1,0:T(1,128)S(1)} %get-tuple-element.8), channel_id=1, source_target_pairs={{1,0},{2,1},{3,2},{4,3},{5,4},{6,5},{7,6},{8,7},{9,8},{10,9},{11,1... | collective-permute-start | bytes 393224 | tf_op jit(solution)/shard_map/ppermute | solution.py:20
  46.2 0.9 copy-start.6
  46.2 83.5 %copy-start.7 = (f32[16,2048]{1,0:T(8,128)S(1)}, f32[16,2048]{1,0:T(8,128)}, u32[]{:S(2)}) copy-start(f32[16,2048]{1,0:T(8,128)} %param.11) | copy-start | bytes 393220
Sparse Core Ops, SparseCore 0:
  48.0 81.6 all-reduce.3
where the time goes:
time: 225 us; the launch traced here: 224 us
  waiting for transfers between devices  88.4 us (39%)
  blocking collectives  82.8 us (37%)
  starting transfers between devices  18.8 us (8%)
  between operations  16.1 us (7%)
  other arithmetic  12 us (5%)
  local copies, waits for them, and re-layouts  6.22 us (3%)
    psum x1, blocking collectives, shards(): curvature = lax.psum(jnp.sum(direction * hessian_product), 'space') / cells  82.8 us
    psum x1, waiting for transfers between devices, shards(): hessian_product = lax.psum(share, 'tm')  81.8 us
    ppermute x3, starting transfers between devices, extended(): lax.ppermute(tail, axis, [(i, (i + 1) % count) for i in range(ends)])  14.9 us
    ppermute x3, waiting for transfers between devices, extended(): lax.ppermute(head, axis, [((i + 1) % count, i) for i in range(ends)])  6.54 us
    unnamed x18, local copies, waits for them, and re-layouts  5.38 us
  transfers between devices with their start and end apart: 7, of which 3 were waited for; matrix products, arithmetic and copies ran while one was open for 3% of the time, Pallas kernels for 0%

commit v1 on v0

--- a/solution.py
+++ b/solution.py
@@ -68,7 +68,7 @@
     column_y = jnp.sum(padded_ty[..., 1:] + padded_ty[..., :-1], axis=(0, 1))
     windows = lax.axis_size("tm")
     share = 0.5 * conduct * (column_x + column_y) / (LAYERS * STEPS * windows)
-    hessian_product = lax.psum(share, "tm")
+    hessian_product = jnp.sum(lax.all_gather(share, "tm"), axis=0)
     cells = height * devices * direction.shape[1]
     curvature = lax.psum(jnp.sum(direction * hessian_product), "space") / cells
     return (hessian_product, curvature)

time: 225 us -> 182 us (0.81)
  waiting for transfers between devices: 88.4 us -> 46.4 us
    psum x1 -> x0, waiting for transfers between devices: 81.8 us -> none  [shards(): hessian_product = lax.psum(share, 'tm')]
    all_gather x0 -> x1, waiting for transfers between devices: none -> 39.9 us  [shards(): hessian_product = jnp.sum(lax.all_gather(share, 'tm'), axis=0)]
    unnamed x18 -> x19, local copies, waits for them, and re-layouts: 5.38 us -> 3.87 us
  transfers between devices with their start and end apart: 7 -> 7, of which waited for: 3 -> 3; matrix products, arithmetic and copies ran while one was open for 3% -> 4% of each run, Pallas kernels for 0% -> 0%
where the time goes in v1:
time: 182 us; the launch traced here: 181 us
  blocking collectives  82.9 us (46%)
  waiting for transfers between devices  46.4 us (25%)
  starting transfers between devices  18.8 us (10%)
  between operations  16.1 us (9%)
  other arithmetic  12.3 us (7%)
  local copies, waits for them, and re-layouts  4.72 us (3%)
    psum x1, blocking collectives, shards(): curvature = lax.psum(jnp.sum(direction * hessian_product), 'space') / cells  82.9 us
    all_gather x1, waiting for transfers between devices, shards(): hessian_product = jnp.sum(lax.all_gather(share, 'tm'), axis=0)  39.9 us
    ppermute x3, starting transfers between devices, extended(): lax.ppermute(tail, axis, [(i, (i + 1) % count) for i in range(ends)])  14.9 us
    ppermute x3, waiting for transfers between devices, extended(): lax.ppermute(head, axis, [((i + 1) % count, i) for i in range(ends)])  6.54 us
    ppermute x3, starting transfers between devices, extended(): lax.ppermute(head, axis, [((i + 1) % count, i) for i in range(ends)])  3.88 us
    unnamed x19, local copies, waits for them, and re-layouts  3.87 us
  transfers between devices with their start and end apart: 7, of which 3 were waited for; matrix products, arithmetic and copies ran while one was open for 4% of the time, Pallas kernels for 0%

profile of v1, /device:TPU:0, one launch (start us, length us, event | category | flops | bytes accessed | tf_op | source)
XLA Modules:
  0.0 181.2 jit_solution(11701703171048602270)
XLA Ops:
  7.2 1.1 exponential_multiply_fusion
  8.4 1.3 collective-permute-start.2
  9.7 4.5 %collective-permute-start.3 = (f32[1,2048]{1,0:T(1,128)S(1)}, f32[1,2048]{1,0:T(1,128)S(1)}, u32[]{:S(2)}, u32[]{:S(2)}) collective-permute-start(f32[1,2048]{1,0:T(1,128)S(1)} %get-tuple-element.10), channel_id=1, source_target_pairs={{0,1},{1,2},{2,3},{3,4},{4,5},{5,6},{6,7},{7,8},{8,9},{9,10},{10,1... | collective-permute-start | bytes 24584 | tf_op jit(solution)/shard_map/ppermute | solution.py:18
  14.2 1.7 constant_dynamic-update-slice_fusion.1
  16.0 0.2 constant_dynamic-update-slice_fusion
  16.2 1.9 %copy-done.2 = f32[2,2,8,16,2048]{4,3,2,1,0:T(8,128)} copy-done((f32[2,2,8,16,2048]{4,3,2,1,0:T(8,128)}, f32[2,2,8,16,2048]{4,3,2,1,0:T(8,128)S(1)}, u32[]{:S(2)}) %copy-start.2) | copy-done | bytes 4194328
  18.2 0.4 fusion.27
  18.6 1.3 collective-permute-start
  19.9 4.6 %collective-permute-start.1 = (f32[2,2,8,1,2048]{4,3,2,1,0:T(1,128)S(1)}, f32[2,2,8,1,2048]{4,3,2,1,0:T(1,128)S(1)}, u32[]{:S(2)}, u32[]{:S(2)}) collective-permute-start(f32[2,2,8,1,2048]{4,3,2,1,0:T(1,128)S(1)} %get-tuple-element.7), channel_id=1, source_target_pairs={{0,1},{1,2},{2,3},{3,4},{4,5},{5,6},{6,7},{7,8},{8,9},{9,10},{10,1... | collective-permute-start | bytes 786440 | tf_op jit(solution)/shard_map/ppermute | solution.py:18
  24.6 3.5 %broadcast_multiply_fusion.1 = (f32[2,8,16,2047]{3,2,1,0:T(8,128)S(1)}, f32[2,8,16,2047]{3,2,1,0:T(8,128)S(1)}) fusion(f32[16,2047]{1,0:T(8,128)S(1)} %fusion.24, f32[2,8,16,2048]{3,2,1,0:T(8,128)S(1)} %bitcast.11, f32[2,8,16,2048]{3,2,1,0:T(8,128)} %bitcast.12), kind=kLoop, calls=%fused_computation.36 | loop fusion | flops 2620160 | bytes 12707776 | tf_op jit(solution)/shard_map/mul | solution.py:42
  28.3 0.4 collective-permute-done
  28.6 1.6 broadcast_multiply_fusion
  30.2 1.1 fusion.14
  31.6 5.8 %collective-permute-start.4 = (f32[2,8,1,2048]{3,2,1,0:T(1,128)S(1)}, f32[2,8,1,2048]{3,2,1,0:T(1,128)S(1)}, u32[]{:S(2)}, u32[]{:S(2)}) collective-permute-start(f32[2,8,1,2048]{3,2,1,0:T(1,128)S(1)} %get-tuple-element.9), channel_id=1, source_target_pairs={{0,1},{1,2},{2,3},{3,4},{4,5},{5,6},{6,7},{7,8},{8,9},{9,10},{10,1... | collective-permute-start | bytes 393224 | tf_op jit(solution)/shard_map/ppermute | solution.py:18
  37.3 1.3 collective-permute-start.5
  38.6 0.8 fusion.17
  39.4 0.6 fusion.16
  40.1 6.2 %collective-permute-done.5 = f32[2,8,1,2048]{3,2,1,0:T(1,128)S(1)} collective-permute-done((f32[2,8,1,2048]{3,2,1,0:T(1,128)S(1)}, f32[2,8,1,2048]{3,2,1,0:T(1,128)S(1)}, u32[]{:S(2)}, u32[]{:S(2)}) %collective-permute-start.5) | collective-permute-done | bytes 131104 | tf_op jit(solution)/shard_map/ppermute | solution.py:20
  46.2 0.7 fusion.9
  47.1 0.7 fusion.23
  47.9 39.9 %all-gather.3.cloned.1.call-done = f32[128,2048]{1,0:T(8,128)} async-done(((f32[16,2048]{1,0:T(8,128)}), f32[128,2048]{1,0:T(8,128)}) %all-gather.3.cloned.1.call-update) | async-done | bytes 1048592 | tf_op jit(solution)/shard_map/all_gather | solution.py:71
  87.7 1.3 reduce_sum.38
  89.0 0.6 multiply_reduce_fusion
  89.7 82.9 %psum.7 = f32[]{:T(128)} all-reduce(f32[]{:T(128)} %multiply_reduce_fusion), channel_id=1, replica_groups=mesh['tm'=8,'space'=32] {'space'}, use_global_device_ids=true, to_apply=%region_4.5 | all-reduce | flops 1 | bytes 8 | tf_op jit(solution)/shard_map/psum | solution.py:73
  (28 shorter events, 0.6 us)
Async XLA Ops:
  7.2 80.6 %all-gather.3.cloned.1.call-start = ((), (), s32[]{:S(2)}) async-start(), calls=%async_computation | async-start | bytes 1179648 | tf_op jit(solution)/shard_map/all_gather | solution.py:71
  7.2 8.8 %copy-start.1 = (f32[1,2,8,16,2048]{4,3,2,1,0:T(8,128)S(1)}, f32[1,2,8,16,2048]{4,3,2,1,0:T(8,128)}, u32[]{:S(2)}) copy-start(f32[1,2,8,16,2048]{4,3,2,1,0:T(8,128)} %param.7) | copy-start | bytes 6291460
  8.4 19.8 %collective-permute-start.2 = (f32[1,2048]{1,0:T(1,128)S(1)}, f32[1,2048]{1,0:T(1,128)S(1)}, u32[]{:S(2)}, u32[]{:S(2)}) collective-permute-start(f32[1,2048]{1,0:T(1,128)S(1)} %get-tuple-element.11), channel_id=1, source_target_pairs={{1,0},{2,1},{3,2},{4,3},{5,4},{6,5},{7,6},{8,7},{9,8},{10,9},{11,1... | collective-permute-start | bytes 24584 | tf_op jit(solution)/shard_map/ppermute | solution.py:20
  9.7 18.5 %collective-permute-start.3 = (f32[1,2048]{1,0:T(1,128)S(1)}, f32[1,2048]{1,0:T(1,128)S(1)}, u32[]{:S(2)}, u32[]{:S(2)}) collective-permute-start(f32[1,2048]{1,0:T(1,128)S(1)} %get-tuple-element.10), channel_id=1, source_target_pairs={{0,1},{1,2},{2,3},{3,4},{4,5},{5,6},{6,7},{7,8},{8,9},{9,10},{10,1... | collective-permute-start | bytes 24584 | tf_op jit(solution)/shard_map/ppermute | solution.py:18
  16.0 8.6 %copy-start = (f32[1,2,8,16,2048]{4,3,2,1,0:T(8,128)S(1)}, f32[1,2,8,16,2048]{4,3,2,1,0:T(8,128)}, u32[]{:S(2)}) copy-start(f32[1,2,8,16,2048]{4,3,2,1,0:T(8,128)} %param.6) | copy-start | bytes 6291460
  16.2 1.9 %copy-start.2 = (f32[2,2,8,16,2048]{4,3,2,1,0:T(8,128)}, f32[2,2,8,16,2048]{4,3,2,1,0:T(8,128)S(1)}, u32[]{:S(2)}) copy-start(f32[2,2,8,16,2048]{4,3,2,1,0:T(8,128)S(1)} %constant_dynamic-update-slice_fusion) | copy-start | bytes 12582916
  18.6 10.0 %collective-permute-start = (f32[2,2,8,1,2048]{4,3,2,1,0:T(1,128)S(1)}, f32[2,2,8,1,2048]{4,3,2,1,0:T(1,128)S(1)}, u32[]{:S(2)}, u32[]{:S(2)}) collective-permute-start(f32[2,2,8,1,2048]{4,3,2,1,0:T(1,128)S(1)} %get-tuple-element.6), channel_id=1, source_target_pairs={{1,0},{2,1},{3,2},{4,3},{5,4},{6,5},{7,6},{8,7},{9,8},{10,9},{11,1... | collective-permute-start | bytes 786440 | tf_op jit(solution)/shard_map/ppermute | solution.py:20
  19.9 8.7 %collective-permute-start.1 = (f32[2,2,8,1,2048]{4,3,2,1,0:T(1,128)S(1)}, f32[2,2,8,1,2048]{4,3,2,1,0:T(1,128)S(1)}, u32[]{:S(2)}, u32[]{:S(2)}) collective-permute-start(f32[2,2,8,1,2048]{4,3,2,1,0:T(1,128)S(1)} %get-tuple-element.7), channel_id=1, source_target_pairs={{0,1},{1,2},{2,3},{3,4},{4,5},{5,6},{6,7},{7,8},{8,9},{9,10},{10,1... | collective-permute-start | bytes 786440 | tf_op jit(solution)/shard_map/ppermute | solution.py:18
  24.6 4.0 %copy-start.3 = (f32[2,2,8,16,2048]{4,3,2,1,0:T(8,128)S(1)}, f32[2,2,8,16,2048]{4,3,2,1,0:T(8,128)}, u32[]{:S(2)}) copy-start(f32[2,2,8,16,2048]{4,3,2,1,0:T(8,128)} %copy-done.2) | copy-start | bytes 12582916
  28.2 2.0 %copy-start.4 = (f32[1,2,8,16,2048]{4,3,2,1,0:T(8,128)S(1)}, f32[1,2,8,16,2048]{4,3,2,1,0:T(8,128)}, u32[]{:S(2)}) copy-start(f32[1,2,8,16,2048]{4,3,2,1,0:T(8,128)} %param.8) | copy-start | bytes 6291460
  28.2 2.0 %copy-start.5 = (f32[1,8,16,2048]{3,2,1,0:T(8,128)S(1)}, f32[1,8,16,2048]{3,2,1,0:T(8,128)}, u32[]{:S(2)}) copy-start(f32[1,8,16,2048]{3,2,1,0:T(8,128)} %param.9) | copy-start | bytes 3145732
  31.6 8.5 %collective-permute-start.4 = (f32[2,8,1,2048]{3,2,1,0:T(1,128)S(1)}, f32[2,8,1,2048]{3,2,1,0:T(1,128)S(1)}, u32[]{:S(2)}, u32[]{:S(2)}) collective-permute-start(f32[2,8,1,2048]{3,2,1,0:T(1,128)S(1)} %get-tuple-element.9), channel_id=1, source_target_pairs={{0,1},{1,2},{2,3},{3,4},{4,5},{5,6},{6,7},{7,8},{8,9},{9,10},{10,1... | collective-permute-start | bytes 393224 | tf_op jit(solution)/shard_map/ppermute | solution.py:18
  37.3 8.9 %collective-permute-start.5 = (f32[2,8,1,2048]{3,2,1,0:T(1,128)S(1)}, f32[2,8,1,2048]{3,2,1,0:T(1,128)S(1)}, u32[]{:S(2)}, u32[]{:S(2)}) collective-permute-start(f32[2,8,1,2048]{3,2,1,0:T(1,128)S(1)} %get-tuple-element.8), channel_id=1, source_target_pairs={{1,0},{2,1},{3,2},{4,3},{5,4},{6,5},{7,6},{8,7},{9,8},{10,9},{11,1... | collective-permute-start | bytes 393224 | tf_op jit(solution)/shard_map/ppermute | solution.py:20
  46.2 0.9 copy-start.6
  46.2 42.8 %copy-start.7 = (f32[16,2048]{1,0:T(8,128)S(1)}, f32[16,2048]{1,0:T(8,128)}, u32[]{:S(2)}) copy-start(f32[16,2048]{1,0:T(8,128)} %param.11) | copy-start | bytes 393220
  89.0 84.2 %copy-start.8 = (f32[16,2048]{1,0:T(8,128)}, f32[16,2048]{1,0:T(8,128)S(1)}, u32[]{:S(2)}) copy-start(f32[16,2048]{1,0:T(8,128)S(1)} %reduce_sum.38) | copy-start | bytes 393220
Sparse Core Ops, SparseCore 0:
  48.0 39.7 all-gather.2
